TPU v7x, 32 devices: a whole 2x2x4 slice. The times are simulated.
32 devices in a mesh: groups: 2 (over y), adapter: 4 (over z), tensor: 4 (over x, core).
Axes of the slice: x: 2, y: 2, z: 4, core: 2. Of those that a mesh axis runs over, the one named last changes fastest.
Arguments:
- normed_layer_inputs: bfloat16 [4, 512, 8192], P(None, ('groups', 'adapter'), 'tensor'), parts along dimension 1, may hold values from -6 to 6
- key_value_weight: bfloat16 [8192, 1024], P('tensor'), may hold values from -0.0625 to 0.0625
- adapter_down_weight: bfloat16 [8, 8192, 128], P(('groups', 'adapter'), 'tensor'), parts along dimension 0, may hold values from -0.0625 to 0.0625
- adapter_up_weight: bfloat16 [8, 2, 64, 512], P(('groups', 'adapter')), parts along dimension 0, may hold values from -0.75 to 0.75
- request_adapter_index: int32 [512, 1], P(('groups', 'adapter')), parts along dimension 0, may hold values from 0 to 3; in each aligned block of 64 rows (0 to 63, 64 to 127, ...) at most 48 rows name the same one
- queries: bfloat16 [4, 512, 4096], P(None, ('groups', 'adapter'), 'tensor'), parts along dimension 1, may hold values from -4.6 to 4.6
- stored_cache_keys: bfloat16 [512, 64, 512], P(('groups', 'adapter', 'tensor')), parts along dimension 0, may hold values from -4.6 to 4.6
- stored_cache_values: bfloat16 [512, 64, 512], P(('groups', 'adapter', 'tensor')), parts along dimension 0, may hold values from -6 to 6
- filled_cache_length: int32 [512], P(('groups', 'adapter', 'tensor')), parts along dimension 0, may hold values from 2 to 64
Outputs:
- context: bfloat16 [4, 512, 4096], P(None, ('groups', 'adapter'), 'tensor'), parts along dimension 1
- new_kv: bfloat16 [4, 512, 1024], P(None, ('groups', 'adapter', 'tensor')), parts along dimension 1
There are 2 independent parts, one for each index of `groups`. A program takes and returns all parts, laid end to end along the dimension named above; an argument that names none is the same for every part. Nothing has to cross between parts.
Inputs may be any that keep to these rules, and one draw needn't show every extreme that they name: `request_adapter_index`: among the 64 requests of each index of the adapter axis no adapter is named more than 48 times, and exactly 48 times in some such block.
All inputs are finite; a program needn't handle non-finite values.
Results may differ from a plain program's by a relative error of at most 0.0057.
Values may be sent and summed in bfloat16 or wider, within the bound.
A program may use at most 64 MiB of HBM per device.

v0:
```python
import math

import jax
import jax.numpy as jnp
from jax import lax
from jax.sharding import PartitionSpec as P

HQ = 32
KV = 4
HD = 128
KEY_VALUE_WIDTH = 512


def rotate_keys(key_rows, positions):
    shaped = key_rows.reshape(key_rows.shape[:-1] + (KV, HD))
    key_width = HD // 2
    pair_index = jnp.arange(key_width, dtype=jnp.float32)
    frequency = jnp.exp(-(2.0 * pair_index / HD) * math.log(500000.0))
    angles = positions[:, :, None, None] * frequency
    cosine = jnp.cos(angles)
    sine = jnp.sin(angles)
    first_half = shaped[..., :key_width]
    second_half = shaped[..., key_width:]
    turned = jnp.concatenate(
        [first_half * cosine - second_half * sine, second_half * cosine + first_half * sine], -1
    )
    return turned.reshape(key_rows.shape)


def attend(query_rows, stored_cache_keys, stored_cache_values, filled_cache_length, new_kv):
    step_count, row_count = (query_rows.shape[0], query_rows.shape[1])
    cache_len = stored_cache_keys.shape[1]
    new_keys = jnp.swapaxes(new_kv[..., :KEY_VALUE_WIDTH], 0, 1)
    new_values = jnp.swapaxes(new_kv[..., KEY_VALUE_WIDTH:], 0, 1)
    all_keys = jnp.concatenate([stored_cache_keys, new_keys], 1)
    all_values = jnp.concatenate([stored_cache_values, new_values], 1)
    span = all_keys.shape[1]
    group_size = HQ // KV
    query_heads = query_rows.reshape(step_count, row_count, KV, group_size, HD)
    key_heads = all_keys.reshape(row_count, span, KV, HD)
    value_heads = all_values.reshape(row_count, span, KV, HD)
    scores = jnp.einsum(
        "srkgd,rpkd->srkgp", query_heads, key_heads, preferred_element_type=jnp.float32
    ) * (1.0 / math.sqrt(HD))
    position = jnp.arange(span, dtype=jnp.int32)
    in_cache = position[None, None, :] < filled_cache_length[None, :, None]
    in_new = (position - cache_len)[None, None, :] <= jnp.arange(step_count, dtype=jnp.int32)[
        :, None, None
    ]
    visible = jnp.where(position[None, None, :] < cache_len, in_cache, in_new)
    scores = jnp.where(visible[:, :, None, None, :], scores, jnp.float32(-1e30))
    row_max = jnp.max(scores, axis=-1, keepdims=True)
    exponent = jnp.exp(scores - row_max)
    totals = jnp.sum(exponent, axis=-1, keepdims=True)
    weights = exponent.astype(jnp.bfloat16)
    context = (
        jnp.einsum("srkgp,rpkd->srkgd", weights, value_heads, preferred_element_type=jnp.float32)
        / totals
    )
    return context.reshape(step_count, row_count, HQ * HD).astype(jnp.bfloat16)


def body(
    normed_layer_inputs,
    key_value_weight,
    adapter_down_weight,
    adapter_up_weight,
    request_adapter_index,
    queries,
    stored_cache_keys,
    stored_cache_values,
    filled_cache_length,
):
    n_adapter = lax.axis_size("adapter")
    n_tensor = lax.axis_size("tensor")
    tensor_index = lax.axis_index("tensor")
    step_count, rows_dev, d_local = normed_layer_inputs.shape
    own_rows = rows_dev // n_tensor
    capacity = max(2, 3 * rows_dev // n_adapter)
    slot_count = n_adapter * capacity
    kv_width = key_value_weight.shape[1]
    partial_value = jnp.dot(
        normed_layer_inputs.reshape(step_count * rows_dev, d_local),
        key_value_weight,
        preferred_element_type=jnp.float32,
    )
    partial_value = partial_value.reshape(step_count, rows_dev, kv_width)
    adapter_of = request_adapter_index[:, 0]
    owners = jnp.arange(n_adapter, dtype=jnp.int32)
    member = (adapter_of[:, None] == owners[None, :]).astype(jnp.int32)
    before = jnp.cumsum(member, axis=0) - member
    slot_index = jnp.sum(before * member, axis=1)
    target = adapter_of * capacity + slot_index
    dispatch = (target[None, :] == jnp.arange(slot_count, dtype=jnp.int32)[:, None]).astype(
        jnp.bfloat16
    )
    outbound_rows = jnp.einsum(
        "qr,srd->qsd", dispatch, normed_layer_inputs, preferred_element_type=jnp.float32
    ).astype(jnp.bfloat16)
    outbound_rows = outbound_rows.reshape(n_adapter, capacity, step_count, d_local)
    slot_block = outbound_rows
    partial_rank_sum = jnp.einsum(
        "kcsd,kdr->kcsr",
        slot_block,
        lax.all_gather(adapter_down_weight, "adapter", axis=0, tiled=True),
        preferred_element_type=jnp.float32,
    )
    reduced_output = lax.psum(partial_rank_sum, "tensor").astype(jnp.bfloat16)
    shard_piece = lax.all_gather(adapter_up_weight, "adapter", axis=0, tiled=True)
    slot_block = reduced_output
    half_of_rank = slot_block.shape[-1] // 2
    key_projection_part = jnp.einsum(
        "kcsr,krv->kcsv",
        slot_block[..., :half_of_rank],
        shard_piece[:, 0],
        preferred_element_type=jnp.float32,
    )
    value_projection_part = jnp.einsum(
        "kcsr,krv->kcsv",
        slot_block[..., half_of_rank:],
        shard_piece[:, 1],
        preferred_element_type=jnp.float32,
    )
    expanded = jnp.concatenate([key_projection_part, value_projection_part], -1)
    returned_delta = expanded.astype(jnp.bfloat16).reshape(slot_count, step_count, kv_width)
    base = lax.psum_scatter(partial_value, "tensor", scatter_dimension=1, tiled=True)
    dispatch_own = lax.dynamic_slice_in_dim(dispatch, tensor_index * own_rows, own_rows, 1)
    delta_rows = jnp.einsum(
        "qr,qsc->src", dispatch_own, returned_delta, preferred_element_type=jnp.float32
    )
    fresh_kv = base + delta_rows
    positions = (
        filled_cache_length[None, :] + jnp.arange(step_count, dtype=jnp.int32)[:, None]
    ).astype(jnp.float32)
    key_width = kv_width // 2
    turned = rotate_keys(fresh_kv[..., :key_width], positions)
    new_kv = jnp.concatenate([turned, fresh_kv[..., key_width:]], -1).astype(jnp.bfloat16)
    query_rows = lax.all_to_all(queries, "tensor", split_axis=1, concat_axis=2, tiled=True)
    context_rows = attend(
        query_rows, stored_cache_keys, stored_cache_values, filled_cache_length, new_kv
    )
    context = lax.all_to_all(context_rows, "tensor", split_axis=2, concat_axis=1, tiled=True)
    return (context, new_kv)


def solution(mesh):
    in_specs = (
        P(None, ("groups", "adapter"), "tensor"),
        P("tensor", None),
        P(("groups", "adapter"), "tensor", None),
        P(("groups", "adapter"), None, None, None),
        P(("groups", "adapter"), None),
        P(None, ("groups", "adapter"), "tensor"),
        P(("groups", "adapter", "tensor"), None, None),
        P(("groups", "adapter", "tensor"), None, None),
        P(("groups", "adapter", "tensor")),
    )
    out_specs = (
        P(None, ("groups", "adapter"), "tensor"),
        P(None, ("groups", "adapter", "tensor"), None),
    )
    return jax.shard_map(body, mesh=mesh, in_specs=in_specs, out_specs=out_specs, check_vma=False)
```

profile of v0, /device:TPU:0, one launch (start us, length us, event | category | flops | bytes accessed | tf_op | source)
XLA Modules:
  0.0 138.0 jit_solution(11034066852912697586)
XLA Ops:
  8.1 0.7 all-gather.2.cloned.1.call-update
  8.7 2.2 %copy.49 = bf16[4,64,1024]{2,0,1:T(4,128)(2,1)} copy(bf16[4,64,1024]{2,1,0:T(8,128)(2,1)} %param.14) | data formatting | bytes 1048576 | tf_op args[5]
  11.0 4.2 %all-to-all-start = ((bf16[4,64,1024]{2,0,1:T(4,128)(2,1)}), bf16[4,64,1024]{2,0,1:T(4,128)(2,1)S(1)}, u32[]{:S(2)}, u32[]{:S(2)}) async-start(bf16[4,64,1024]{2,0,1:T(4,128)(2,1)} %copy.49), calls=%async_computation.1 | async-start | bytes 1048576 | tf_op jit(solution)/shard_map/all_to_all | solution.py:138
  15.3 4.5 %fusion = f32[4,64,1024]{2,1,0:T(8,128)} fusion(bf16[4,64,2048]{2,1,0:T(8,128)(2,1)S(1)} %copy-done, bf16[2048,1024]{1,0:T(8,128)(2,1)} %param.10), kind=kOutput, calls=%fused_computation | convolution fusion | flops 1073741824 | bytes 6291456 | tf_op jit(solution)/shard_map/dot_general | solution.py:82
  20.6 23.6 %all_gather.7 = bf16[4,2,64,512]{3,2,0,1:T(8,128)(2,1)S(1)} all-gather(bf16[1,2,64,512]{3,2,0,1:T(8,128)(2,1)S(1)} %bitcast.79), channel_id=1, replica_groups=mesh['groups'=2,'adapter'=4,'tensor'=4] {'adapter'}, dimensions={0}, use_global_device_ids=true | all-gather | bytes 655360 | tf_op jit(solution)/shard_map/all_gather | solution.py:109
  44.2 2.7 %convolution_convert_fusion = bf16[192,4,2048]{2,0,1:T(8,128)(2,1)} fusion(bf16[4,64,2048]{2,1,0:T(8,128)(2,1)S(1)} %copy-done, s32[64]{0:T(128)S(1)} %multiply_add_fusion), kind=kOutput, calls=%fused_computation.2 | convolution fusion | flops 202911744 | bytes 4194560 | tf_op jit(solution)/shard_map/qr,srd->qsd/dot_general | solution.py:97
  47.2 1.0 reshape.140
  48.2 19.4 %all-gather.2.cloned.1.call-done = bf16[4,2048,128]{2,1,0:T(8,128)(2,1)} async-done(((bf16[1,2048,128]{2,1,0:T(8,128)(2,1)}), bf16[4,2048,128]{2,1,0:T(8,128)(2,1)}) %all-gather.2.cloned.1.call-update) | async-done | bytes 2097168 | tf_op jit(solution)/shard_map/all_gather | solution.py:105
  67.5 3.5 %fusion.2 = f32[4,48,4,128]{3,1,2,0:T(8,128)S(1)} fusion(bf16[4,48,4,2048]{3,1,0,2:T(8,128)(2,1)} %bitcast.70, bf16[4,2048,128]{2,1,0:T(8,128)(2,1)} %all-gather.2.cloned.1.call-done), kind=kOutput, calls=%fused_computation.3 | convolution fusion | flops 402653184 | bytes 5636096 | tf_op jit(solution)/shard_map/kcsd,kdr->kcsr/dot_general | solution.py:102
  71.1 15.3 %all-reduce.1 = bf16[4,48,4,128]{3,1,2,0:T(8,128)(2,1)S(1)} all-reduce(f32[4,48,4,128]{3,1,2,0:T(8,128)S(1)} %fusion.2), channel_id=1, replica_groups=mesh['groups'=2,'adapter'=4,'tensor'=4] {'tensor'}, use_global_device_ids=true, to_apply=%region_3.4 | all-reduce | flops 98304 | bytes 589824 | tf_op jit(solution)/shard_map/psum | solution.py:108
  87.2 1.0 copy.44
  88.2 1.6 %fusion.18 = f32[4,16,1024]{2,1,0:T(8,128)S(1)} fusion(f32[4,16,1024]{2,1,0:T(8,128)} %reduce-scatter.2.cloned.1.call-done, bf16[192,4,512]{2,0,1:T(8,128)(2,1)} %bitcast.76, bf16[192,4,512]{2,0,1:T(8,128)(2,1)S(1)} %bitcast.75, pred[192,64]{0,1:T(8,128)(4,1)S(1)} %iota_compare_fusion, s32[]{:T(128)S(6)} %select_n.15), kind=kOutput, calls=%fused_computation.23 | convolution fusion | flops 28377088 | bytes 2101252 | tf_op jit(solution)/shard_map/qr,qsc->src/dot_general | solution.py:128
  91.6 1.3 pad_maximum_fusion
  92.9 1.2 reshape.149
  94.1 2.0 %fusion.33 = (f32[4,16,4,8]{3,0,2,1:T(4,128)S(1)}, f32[4,16,4,8,68]{4,3,0,2,1:T(8,128)S(1)}) fusion(bf16[4,16,4,8,128]{4,3,0,2,1:T(8,128)(2,1)} %reshape.140, bf16[16,68,4,128,1]{3,2,1,0,4:T(4,128)(2,1)S(1)} %bitcast.73, pred[4,16,68]{2,0,1:T(4,128)(4,1)S(1)} %broadcast_select_fusion), kind=kOutput, calls=%fused_computation.57 | convolution fusion | flops 36067328 | bytes 2208000 | tf_op jit(solution)/shard_map/srkgd,rpkd->srkgp/dot_general | solution.py:42
  96.1 0.8 fusion.21
  96.9 0.8 fusion.12
  97.7 3.5 %copy.70 = bf16[4,16,4,8,128]{1,0,4,3,2:T(4,128)(2,1)} copy(bf16[4,16,4,8,128]{4,3,0,2,1:T(8,128)(2,1)S(1)} %fusion.12) | data formatting | bytes 1048576 | tf_op jit(solution)/shard_map/convert_element_type | solution.py:60
  101.2 6.5 %reshape.151 = bf16[4,2,32768]{2,1,0:T(2,128)(2,1)} reshape(bf16[4096,4,16]{2,1,0:T(4,128)(2,1)} %bitcast.68) | data formatting | bytes 1048576
  107.6 3.5 %all-to-all-start.1 = ((bf16[4,2,32768]{2,1,0:T(2,128)(2,1)}), bf16[4,2,32768]{2,1,0:T(2,128)(2,1)S(1)}, u32[]{:S(2)}, u32[]{:S(2)}) async-start(bf16[4,2,32768]{2,1,0:T(2,128)(2,1)} %reshape.151), calls=%async_computation.2 | async-start | bytes 1048576 | tf_op jit(solution)/shard_map/all_to_all | solution.py:142
  111.1 0.9 slice.56
  112.7 7.2 %all-to-all-done.1 = bf16[4,2,32768]{2,1,0:T(2,128)(2,1)S(1)} async-done(((bf16[4,2,32768]{2,1,0:T(2,128)(2,1)}), bf16[4,2,32768]{2,1,0:T(2,128)(2,1)S(1)}, u32[]{:S(2)}, u32[]{:S(2)}) %all-to-all-start.1) | async-done | bytes 524320 | tf_op jit(solution)/shard_map/all_to_all | solution.py:142
  119.9 4.1 %reshape.152 = bf16[4096,4,16]{2,1,0:T(4,128)(2,1)} reshape(bf16[4,2,32768]{2,1,0:T(2,128)(2,1)S(1)} %all-to-all-done.1) | data formatting | bytes 1048576
  124.0 6.6 %copy.56 = bf16[4,4,16,1024]{3,2,1,0:T(8,128)(2,1)} copy(bf16[4,4,16,1024]{2,0,3,1:T(4,128)(2,1)} %bitcast.69) | data formatting | bytes 1048576 | tf_op jit(solution)/shard_map/all_to_all | solution.py:142
  (47 shorter events, 4.3 us)
Async XLA Ops:
  8.0 7.3 %copy-start = (bf16[4,64,2048]{2,1,0:T(8,128)(2,1)S(1)}, bf16[4,64,2048]{2,1,0:T(8,128)(2,1)}, u32[]{:S(2)}) copy-start(bf16[4,64,2048]{2,1,0:T(8,128)(2,1)} %param.9) | copy-start | bytes 3145732
  8.0 59.5 %all-gather.2.cloned.1.call-start = ((), (), s32[]{:S(2)}) async-start(), calls=%async_computation.4 | async-start | bytes 2621440 | tf_op jit(solution)/shard_map/all_gather | solution.py:105
  11.0 35.9 %all-to-all-start = ((bf16[4,64,1024]{2,0,1:T(4,128)(2,1)}), bf16[4,64,1024]{2,0,1:T(4,128)(2,1)S(1)}, u32[]{:S(2)}, u32[]{:S(2)}) async-start(bf16[4,64,1024]{2,0,1:T(4,128)(2,1)} %copy.49), calls=%async_computation.1 | async-start | bytes 1048576 | tf_op jit(solution)/shard_map/all_to_all | solution.py:138
  15.2 4.6 %copy-start.6 = (s32[16]{0:T(128)S(1)}, s32[16]{0:T(128)}, u32[]{:S(2)}) copy-start(s32[16]{0:T(128)} %param.17) | copy-start | bytes 196
  15.2 4.7 %copy-start.5 = (s32[64,1]{0,1:T(1,128)S(1)}, s32[64,1]{0,1:T(1,128)}, u32[]{:S(2)}) copy-start(s32[64,1]{0,1:T(1,128)} %param.13) | copy-start | bytes 772
  15.2 5.4 %copy-start.4 = (bf16[1,2,64,512]{3,2,1,0:T(8,128)(2,1)S(1)}, bf16[1,2,64,512]{3,2,1,0:T(8,128)(2,1)}, u32[]{:S(2)}) copy-start(bf16[1,2,64,512]{3,2,1,0:T(8,128)(2,1)} %param.12) | copy-start | bytes 393220
  15.2 73.0 %reduce-scatter.2.cloned.1.call-start = ((), (), s32[]{:S(2)}) async-start(), calls=%async_computation.3 | async-start | bytes 1310720 | tf_op jit(solution)/shard_map/reduce_scatter | solution.py:126
  88.2 2.8 %copy-start.2 = (bf16[16,64,512]{2,1,0:T(8,128)(2,1)S(1)}, bf16[16,64,512]{2,1,0:T(8,128)(2,1)}, u32[]{:S(2)}) copy-start(bf16[16,64,512]{2,1,0:T(8,128)(2,1)} %param.15) | copy-start | bytes 3145732
  89.8 0.7 copy-start.3
  94.1 2.8 %copy-start.1 = (bf16[16,68,4,128]{3,2,1,0:T(4,128)(2,1)S(1)}, bf16[16,68,4,128]{3,2,1,0:T(4,128)(2,1)}, u32[]{:S(2)}) copy-start(bf16[16,68,4,128]{3,2,1,0:T(4,128)(2,1)} %reshape.149) | copy-start | bytes 3342340
  107.6 12.3 %all-to-all-start.1 = ((bf16[4,2,32768]{2,1,0:T(2,128)(2,1)}), bf16[4,2,32768]{2,1,0:T(2,128)(2,1)S(1)}, u32[]{:S(2)}, u32[]{:S(2)}) async-start(bf16[4,2,32768]{2,1,0:T(2,128)(2,1)} %reshape.151), calls=%async_computation.2 | async-start | bytes 1048576 | tf_op jit(solution)/shard_map/all_to_all | solution.py:142
Sparse Core Ops, SparseCore 0:
  10.5 56.9 all-gather.1
Sparse Core Ops, SparseCore 1:
  19.8 27.3 reduce-scatter.1
where the time goes:
time: 139 us; the launch traced here: 138 us
  blocking collectives  38.9 us (28%)
  local copies, waits for them, and re-layouts  28.6 us (21%)
  waiting for transfers between devices  27.3 us (20%)
  matrix products  15.8 us (11%)
  between operations  15.7 us (11%)
  starting transfers between devices  7.76 us (6%)
  other arithmetic  3.93 us (3%)
    all_gather x1, blocking collectives, body(): lax.all_gather(adapter_up_weight, 'adapter', axis=0, tiled=True)  23.6 us
    all_gather x1, waiting for transfers between devices, body(): lax.all_gather(adapter_down_weight, 'adapter', axis=0, tiled=True)  19.4 us
    psum x1, blocking collectives, body(): reduced_output = lax.psum(partial_rank_sum, 'tensor').astype(jnp.bfloat16)  15.3 us
    unnamed x17, local copies, waits for them, and re-layouts  13.5 us
    all_to_all x1, waiting for transfers between devices, body(): lax.all_to_all(context_rows, 'tensor', split_axis=2, concat_axis=1, tiled...  7.23 us
    all_to_all x1, local copies, waits for them, and re-layouts, body(): lax.all_to_all(context_rows, 'tensor', split_axis=2, concat_axis=1, tiled...  6.56 us
    dot_general x1, matrix products, body(): jnp.dot(normed_layer_inputs.reshape(step_count * rows_dev, d_local), key_...  4.47 us
    all_to_all x1, starting transfers between devices, body(): lax.all_to_all(queries, 'tensor', split_axis=1, concat_axis=2, tiled=True)  4.21 us
  transfers between devices with their start and end apart: 4, of which 2 were waited for; matrix products, arithmetic and copies ran while one was open for 13% of the time, Pallas kernels for 0%

commit v1 on v0

v1 whole, which is shorter than its diff:
```python
import functools
import math

import jax
import jax.numpy as jnp
import numpy as np
from jax import lax
from jax.experimental import pallas as pl
from jax.experimental.pallas import tpu as pltpu
from jax.sharding import PartitionSpec as P

HQ = 32
KV = 4
HD = 128
KEY_VALUE_WIDTH = 512
GROUP = HQ // KV
MESH = pl.DeviceIdType.MESH
F32 = jnp.float32
BF16 = jnp.bfloat16


def kernel(
    n_a, n_t, chunks,
    idx_ref, cos_ref, sin_ref, colok_ref, same_ref, perm_ref,
    x_hbm, w_hbm, a_hbm, u_hbm, q_hbm, k_hbm, v_hbm,
    ctx_hbm, new_ref,
    x_ref, w_ref, down, up, k_ref, v_ref, q_all, qp,
    part, base_in, shr, shr_in, newp, ctxs,
    loc, a_send, a_recv, u_send, u_recv, uz_send, uz_recv,
    q_send, q_recv, b_send, b_recv, s_send, s_recv, c_send, c_recv,
):
    z = lax.axis_index("adapter")
    t = lax.axis_index("tensor")
    steps, rows, depth = x_ref.shape
    own = rows // n_t
    width = w_ref.shape[1]
    tile = steps * rows
    otile = steps * own
    cd = depth // chunks
    uq = up.shape[2]
    hl = q_hbm.shape[2]
    hpt = hl // HD

    x_cp = pltpu.make_async_copy(x_hbm, x_ref, loc.at[0])
    w_cp = pltpu.make_async_copy(w_hbm, w_ref, loc.at[1])
    a_cp = pltpu.make_async_copy(a_hbm.at[0], down.at[z], loc.at[2])
    u_cp = pltpu.make_async_copy(u_hbm.at[t], up.at[z, t], loc.at[3])
    q_cp = pltpu.make_async_copy(
        q_hbm.at[:, pl.ds(pl.multiple_of(t * own, own), own)], q_all.at[t], loc.at[4])
    k_cp = pltpu.make_async_copy(k_hbm, k_ref, loc.at[5])
    v_cp = pltpu.make_async_copy(v_hbm, v_ref, loc.at[6])
    for cp in (a_cp, u_cp, x_cp, w_cp, q_cp, k_cp, v_cp):
        cp.start()

    barrier = pltpu.get_barrier_semaphore()
    for d in range(1, n_t):
        pl.semaphore_signal(barrier, inc=1, device_id={"tensor": lax.rem(t + d, n_t)}, device_id_type=MESH)

    @pl.when(z > 0)
    def _():
        pl.semaphore_signal(barrier, inc=1, device_id={"adapter": z - 1}, device_id_type=MESH)

    @pl.when(z < n_a - 1)
    def _():
        pl.semaphore_signal(barrier, inc=1, device_id={"adapter": z + 1}, device_id_type=MESH)

    pl.semaphore_wait(barrier, n_t - 1 + jnp.where(z > 0, 1, 0) + jnp.where(z < n_a - 1, 1, 0))

    def a_copy(direction, k, c):
        a = z - k if direction == 0 else z + k
        to = z + 1 if direction == 0 else z - 1
        block = down.at[a, pl.ds(c * cd, cd)]
        return pltpu.make_async_remote_copy(
            src_ref=block, dst_ref=block, send_sem=a_send.at[direction, k, c],
            recv_sem=a_recv.at[direction, k, c], device_id={"adapter": to}, device_id_type=MESH)

    def uz_copy(direction, k):
        a = z - k if direction == 0 else z + k
        to = z + 1 if direction == 0 else z - 1
        block = up.at[a, t]
        return pltpu.make_async_remote_copy(
            src_ref=block, dst_ref=block, send_sem=uz_send.at[direction, k],
            recv_sem=uz_recv.at[direction, k], device_id={"adapter": to}, device_id_type=MESH)

    def held(direction, k):
        return z >= k if direction == 0 else z + k < n_a

    def sends(direction, k):
        return jnp.logical_and(held(direction, k), z < n_a - 1 if direction == 0 else z > 0)

    def u_copy(a, slot, d):
        block = up.at[a, t]
        return pltpu.make_async_remote_copy(
            src_ref=block, dst_ref=block, send_sem=u_send.at[slot, d - 1],
            recv_sem=u_recv.at[slot, d - 1], device_id={"tensor": lax.rem(t + d, n_t)}, device_id_type=MESH)

    def arrived_a(direction, k, c):
        a = z - k if direction == 0 else z + k
        block = down.at[a, pl.ds(c * cd, cd)]
        pltpu.make_async_copy(block, block, a_recv.at[direction, k - 1, c]).wait()

    def arrived_uz(direction, k):
        a = z - k if direction == 0 else z + k
        block = up.at[a, t]
        pltpu.make_async_copy(block, block, uz_recv.at[direction, k - 1]).wait()

    u_cp.wait()
    for direction in range(2):
        @pl.when(sends(direction, 0))
        def _(direction=direction):
            uz_copy(direction, 0).start()
    a_cp.wait()
    for c in range(chunks):
        for direction in range(2):
            @pl.when(sends(direction, 0))
            def _(direction=direction, c=c):
                a_copy(direction, 0, c).start()

    def q_copy(d):
        to = lax.rem(t + d, n_t)
        return pltpu.make_async_remote_copy(
            src_ref=q_hbm.at[:, pl.ds(pl.multiple_of(to * own, own), own)], dst_ref=q_all.at[t],
            send_sem=q_send.at[d - 1], recv_sem=q_recv.at[d - 1], device_id={"tensor": to}, device_id_type=MESH)

    def b_copy(d):
        to = lax.rem(t + d, n_t)
        return pltpu.make_async_remote_copy(
            src_ref=part.at[:, pl.ds(pl.multiple_of(to * own, own), own)], dst_ref=base_in.at[d - 1],
            send_sem=b_send.at[d - 1], recv_sem=b_recv.at[d - 1], device_id={"tensor": to}, device_id_type=MESH)

    def s_copy(d):
        to = lax.rem(t + d, n_t)
        return pltpu.make_async_remote_copy(
            src_ref=shr.at[:, pl.ds(pl.multiple_of(to * own, own), own)], dst_ref=shr_in.at[d - 1],
            send_sem=s_send.at[d - 1], recv_sem=s_recv.at[d - 1], device_id={"tensor": to}, device_id_type=MESH)

    for d in range(1, n_t):
        u_copy(z, 0, d).start()
        q_copy(d).start()

    x_cp.wait()
    w_cp.wait()
    bn = 256

    def base_step(i, carry):
        cols = pl.ds(pl.multiple_of(i * bn, bn), bn)
        part[:, :, cols] = jnp.dot(
            x_ref[...].reshape(tile, depth), w_ref[:, cols], preferred_element_type=F32
        ).reshape(steps, rows, bn)
        return carry

    lax.fori_loop(0, width // bn, base_step, 0)
    for d in range(1, n_t):
        b_copy(d).start()

    idx = jnp.concatenate([idx_ref[...]] * steps, axis=0)
    rank = down.shape[2]

    def shrink_part(a, lo, size):
        got = jnp.dot(
            x_ref[:, :, pl.ds(lo, size)].reshape(tile, size), down[a, pl.ds(lo, size)],
            preferred_element_type=F32)
        return jnp.where(idx == a, got, 0.0).reshape(steps, rows, rank)

    shr[...] = shrink_part(z, 0, depth)

    for k in range(1, n_a):
        for direction in range(2):
            @pl.when(held(direction, k))
            def _(direction=direction, k=k):
                arrived_uz(direction, k)
                a = z - k if direction == 0 else z + k
                for d in range(1, n_t):
                    u_copy(a, 2 * k - 1 + direction, d).start()

            @pl.when(sends(direction, k))
            def _(direction=direction, k=k):
                uz_copy(direction, k).start()
        for c in range(chunks):
            for direction in range(2):
                @pl.when(held(direction, k))
                def _(direction=direction, k=k, c=c):
                    arrived_a(direction, k, c)

                @pl.when(sends(direction, k))
                def _(direction=direction, k=k, c=c):
                    a_copy(direction, k, c).start()

            for direction in range(2):
                @pl.when(held(direction, k))
                def _(direction=direction, k=k, c=c):
                    a = z - k if direction == 0 else z + k
                    shr[...] += shrink_part(a, c * cd, cd)

        if k == n_a - 2 or n_a == 2:
            q_cp.wait()
            for d in range(1, n_t):
                q_copy(d).wait()
            for j in range(n_t):
                qp[j] = jnp.dot(
                    perm_ref[...], q_all[j].reshape(otile, hl), preferred_element_type=F32).astype(BF16)
            for d in range(1, n_t):
                b_copy(d).wait()
            mine = pl.ds(pl.multiple_of(t * own, own), own)
            total = part[:, mine]
            for d in range(1, n_t):
                total = total + base_in[d - 1]
            base_in[0] = total
            k_cp.wait()
            v_cp.wait()

    for d in range(1, n_t):
        s_copy(d).start()
    for d in range(1, n_t):
        u_copy(z, 0, d).wait()
    for k in range(1, n_a):
        for direction in range(2):
            @pl.when(held(direction, k))
            def _(direction=direction, k=k):
                a = z - k if direction == 0 else z + k
                for d in range(1, n_t):
                    u_copy(a, 2 * k - 1 + direction, d).wait()
    for d in range(1, n_t):
        s_copy(d).wait()
    mine = pl.ds(pl.multiple_of(t * own, own), own)
    total = shr[:, mine]
    for d in range(1, n_t):
        total = total + shr_in[d - 1]
    shrunk = total.reshape(otile, rank)
    both = jnp.concatenate([shrunk, shrunk], axis=0)
    line = lax.broadcasted_iota(jnp.int32, (2 * otile, rank), 0)
    lane = lax.broadcasted_iota(jnp.int32, (2 * otile, rank), 1)
    both = jnp.where((line < otile) == (lane < rank // 2), both, 0.0)
    idx_own = idx_ref[mine]
    idx_both = jnp.concatenate([idx_own] * (2 * steps), axis=0)
    delta = jnp.zeros((2 * otile, KEY_VALUE_WIDTH), F32)
    for a in range(n_a):
        delta = delta + jnp.dot(
            jnp.where(idx_both == a, both, 0.0).astype(BF16),
            up[a].reshape(rank, KEY_VALUE_WIDTH), preferred_element_type=F32)
    delta = delta.astype(BF16).astype(F32)
    fresh = base_in[0].reshape(otile, width)
    pieces = []
    for h in range(KV):
        one = fresh[:, h * HD:(h + 1) * HD] + delta[:otile, h * HD:(h + 1) * HD]
        pieces.append(one * cos_ref[...] + pltpu.roll(one, HD // 2, 1) * sin_ref[...])
    pieces.append(fresh[:, KEY_VALUE_WIDTH:] + delta[otile:])
    new_kv = jnp.concatenate(pieces, axis=1).astype(BF16)
    new_ref[...] = new_kv.reshape(steps, own, width)
    newp[...] = jnp.dot(perm_ref[...], new_kv, preferred_element_type=F32).astype(BF16)

    def c_copy(d):
        to = lax.rem(t + d, n_t)
        return pltpu.make_async_remote_copy(
            src_ref=ctxs.at[d], dst_ref=ctx_hbm.at[:, pl.ds(pl.multiple_of(t * own, own), own)],
            send_sem=c_send.at[d - 1], recv_sem=c_recv.at[d - 1], device_id={"tensor": to}, device_id_type=MESH)

    per = same_ref.shape[1] // (k_ref.shape[1] + steps)
    scale = 1.0 / math.sqrt(HD)
    order = [n_t // 2] + [d for d in range(1, n_t) if d != n_t // 2] + [0]
    for d in order:
        to = lax.rem(t + d, n_t)
        g = to * hpt // GROUP
        kl = pl.ds(pl.multiple_of(g * HD, HD), HD)
        vl = pl.ds(pl.multiple_of(KEY_VALUE_WIDTH + g * HD, HD), HD)
        tiles = []
        for b in range(own // per):
            r0, n0 = b * per, per * steps
            lines = pl.ds(b * n0, n0)
            qt = jnp.concatenate([qp[to, lines, h * HD:(h + 1) * HD] for h in range(hpt)], axis=0)
            keys = jnp.concatenate(
                [k_ref[pl.ds(r0, per), :, kl].reshape(per * k_ref.shape[1], HD), newp[lines, kl]], axis=0)
            vals = jnp.concatenate(
                [v_ref[pl.ds(r0, per), :, kl].reshape(per * v_ref.shape[1], HD), newp[lines, vl]], axis=0)
            sc = lax.dot_general(qt, keys, (((1,), (1,)), ((), ())), preferred_element_type=F32) * scale
            sc = jnp.where(same_ref[...] * colok_ref[pl.ds(b, 1), :] > 0, sc, -1e30)
            e = jnp.exp(sc - jnp.max(sc, axis=1, keepdims=True))
            tot = jnp.sum(e, axis=1, keepdims=True)
            o = (jnp.dot(e.astype(BF16), vals, preferred_element_type=F32) / tot).astype(BF16)
            tiles.append(jnp.concatenate([o[h * n0:(h + 1) * n0] for h in range(hpt)], axis=1))
        ctxp = jnp.concatenate(tiles, axis=0)
        ctxs[d] = lax.dot_general(
            perm_ref[...], ctxp, (((0,), (0,)), ((), ())), preferred_element_type=F32
        ).astype(BF16).reshape(steps, own, hl)
        if d:
            c_copy(d).start()
    own_cp = pltpu.make_async_copy(ctxs.at[0], ctx_hbm.at[:, mine], loc.at[7])
    own_cp.start()

    for k in range(n_a):
        for direction in range(2):
            @pl.when(sends(direction, k))
            def _(direction=direction, k=k):
                uz_copy(direction, k).wait_send()
                for c in range(chunks):
                    a_copy(direction, k, c).wait_send()
    own_cp.wait()
    for d in range(1, n_t):
        c_copy(d).wait()


def body(
    normed_layer_inputs, key_value_weight, adapter_down_weight, adapter_up_weight,
    request_adapter_index, queries, stored_cache_keys, stored_cache_values, filled_cache_length,
):
    n_a = lax.axis_size("adapter")
    n_t = lax.axis_size("tensor")
    steps, rows, depth = normed_layer_inputs.shape
    own = rows // n_t
    otile = steps * own
    width = key_value_weight.shape[1]
    rank = adapter_down_weight.shape[2]
    cache = stored_cache_keys.shape[1]
    hl = queries.shape[2]
    hpt = hl // HD
    per = 16 // steps
    chunks = 4
    uq = rank // n_t

    i = np.arange(otile)
    perm = np.zeros((otile, otile), np.float32)
    perm[i, (i % steps) * own + i // steps] = 1
    line = np.arange(hpt * per * steps) % (per * steps)
    col_r = np.concatenate([np.repeat(np.arange(per), cache), np.repeat(np.arange(per), steps)])
    col_s = np.concatenate([np.full(per * cache, -1), np.tile(np.arange(steps), per)])
    same = (line[:, None] // steps == col_r[None]) & (col_s[None] <= line[:, None] % steps)
    filled = (jnp.arange(cache, dtype=jnp.int32)[None] < filled_cache_length[:, None]).astype(F32)
    colok = jnp.concatenate(
        [filled.reshape(own // per, per * cache), jnp.ones((own // per, per * steps), F32)], axis=1)
    idx = jnp.broadcast_to(request_adapter_index, (rows, rank))
    positions = (
        filled_cache_length[None, :] + jnp.arange(steps, dtype=jnp.int32)[:, None]
    ).astype(F32).reshape(otile, 1)
    half = HD // 2
    pair = jnp.arange(HD, dtype=jnp.int32) % half
    frequency = jnp.exp(-(2.0 * pair.astype(F32) / HD) * math.log(500000.0))
    angles = positions * frequency[None]
    cosine = jnp.cos(angles)
    sine = jnp.where(jnp.arange(HD)[None] < half, -jnp.sin(angles), jnp.sin(angles))

    vm = pl.BlockSpec(memory_space=pltpu.VMEM)
    hbm = pl.BlockSpec(memory_space=pl.ANY)
    dma = pltpu.SemaphoreType.DMA
    context, new_kv = pl.pallas_call(
        functools.partial(kernel, n_a, n_t, chunks),
        out_shape=(
            jax.ShapeDtypeStruct((steps, rows, hl), BF16),
            jax.ShapeDtypeStruct((steps, own, width), BF16),
        ),
        in_specs=[vm] * 6 + [hbm] * 7,
        out_specs=(hbm, vm),
        scratch_shapes=[
            pltpu.VMEM((steps, rows, depth), BF16),
            pltpu.VMEM((depth, width), BF16),
            pltpu.VMEM((n_a, depth, rank), BF16),
            pltpu.VMEM((n_a, n_t, uq, KEY_VALUE_WIDTH), BF16),
            pltpu.VMEM(stored_cache_keys.shape, BF16),
            pltpu.VMEM(stored_cache_values.shape, BF16),
            pltpu.VMEM((n_t, steps, own, hl), BF16),
            pltpu.VMEM((n_t, otile, hl), BF16),
            pltpu.VMEM((steps, rows, width), F32),
            pltpu.VMEM((n_t - 1, steps, own, width), F32),
            pltpu.VMEM((steps, rows, rank), F32),
            pltpu.VMEM((n_t - 1, steps, own, rank), F32),
            pltpu.VMEM((otile, width), BF16),
            pltpu.VMEM((n_t, steps, own, hl), BF16),
            dma((8,)),
            dma((2, n_a, chunks)), dma((2, n_a, chunks)),
            dma((2 * n_a, n_t - 1)), dma((2 * n_a, n_t - 1)),
            dma((2, n_a)), dma((2, n_a)),
            dma((n_t - 1,)), dma((n_t - 1,)),
            dma((n_t - 1,)), dma((n_t - 1,)),
            dma((n_t - 1,)), dma((n_t - 1,)),
            dma((n_t - 1,)), dma((n_t - 1,)),
        ],
        compiler_params=pltpu.CompilerParams(
            collective_id=0, has_side_effects=True, vmem_limit_bytes=48 * 1024 * 1024),
    )(
        idx, cosine, sine, colok, jnp.asarray(same, F32), jnp.asarray(perm, BF16),
        normed_layer_inputs, key_value_weight, adapter_down_weight,
        adapter_up_weight.reshape(n_t, uq, KEY_VALUE_WIDTH), queries,
        stored_cache_keys, stored_cache_values,
    )
    return (context, new_kv)


def solution(mesh):
    in_specs = (
        P(None, ("groups", "adapter"), "tensor"),
        P("tensor", None),
        P(("groups", "adapter"), "tensor", None),
        P(("groups", "adapter"), None, None, None),
        P(("groups", "adapter"), None),
        P(None, ("groups", "adapter"), "tensor"),
        P(("groups", "adapter", "tensor"), None, None),
        P(("groups", "adapter", "tensor"), None, None),
        P(("groups", "adapter", "tensor")),
    )
    out_specs = (
        P(None, ("groups", "adapter"), "tensor"),
        P(None, ("groups", "adapter", "tensor"), None),
    )
    return jax.shard_map(body, mesh=mesh, in_specs=in_specs, out_specs=out_specs, check_vma=False)
```

time: 139 us -> 68.8 us (0.49)
  Pallas kernels: 0 us -> 55.2 us
  blocking collectives: 38.9 us -> 0 us
  waiting for transfers between devices: 27.3 us -> 0 us
  local copies, waits for them, and re-layouts: 28.6 us -> 11.5 us
  matrix products: 15.8 us -> 0 us
  between operations: 15.7 us -> 0.68 us
  starting transfers between devices: 7.76 us -> 0 us
  other arithmetic: 3.93 us -> 0.89 us
    pallas_call x0 -> x1, Pallas kernels: none -> 55.2 us  [body(): pl.pallas_call(functools.partial(kernel, n_a, n_t, chunks), out_shape=(ja...]
    all_gather x1 -> x0, blocking collectives: 23.6 us -> none  [body(): lax.all_gather(adapter_up_weight, 'adapter', axis=0, tiled=True)]
    all_gather x1 -> x0, waiting for transfers between devices: 19.4 us -> none  [body(): lax.all_gather(adapter_down_weight, 'adapter', axis=0, tiled=True)]
    dot_general x8 -> x0, matrix products: 15.8 us -> none  [the longest x1 4.47 us: body(): jnp.dot(normed_layer_inputs.reshape(step_count * rows_dev, d_local), key_...]
    psum x1 -> x0, blocking collectives: 15.3 us -> none  [body(): reduced_output = lax.psum(partial_rank_sum, 'tensor').astype(jnp.bfloat16)]
    all_to_all x2 -> x0, starting transfers between devices: 7.68 us -> none  [the longest x1 4.21 us: body(): lax.all_to_all(queries, 'tensor', split_axis=1, concat_axis=2, tiled=True)]
    all_to_all x2 -> x0, waiting for transfers between devices: 7.23 us -> none  [the longest x1 7.23 us: body(): lax.all_to_all(context_rows, 'tensor', split_axis=2, concat_axis=1, tiled...]
    all_to_all x2 -> x0, local copies, waits for them, and re-layouts: 6.79 us -> none  [the longest x1 6.56 us: body(): lax.all_to_all(context_rows, 'tensor', split_axis=2, concat_axis=1, tiled...]
  transfers between devices with their start and end apart: 4 -> 0, of which waited for: 2 -> 0; matrix products, arithmetic and copies ran while one was open for 13% -> 0% of each run, Pallas kernels for 0% -> 0%
where the time goes in v1:
time: 68.8 us; the launch traced here: 68.4 us
  Pallas kernels  55.2 us (80%)
  local copies, waits for them, and re-layouts  11.5 us (17%)
  other arithmetic  0.89 us (1%)
    pallas_call x1, Pallas kernels, body(): pl.pallas_call(functools.partial(kernel, n_a, n_t, chunks), out_shape=(ja...  55.2 us
    unnamed x18, local copies, waits for them, and re-layouts  9.75 us

profile of v1, /device:TPU:0, one launch (start us, length us, event | category | flops | bytes accessed | tf_op | source)
XLA Modules:
  0.0 68.4 jit_solution(7509239207487271751)
XLA Ops:
  0.7 0.7 %lt.42 = s32[4,4]{1,0:T(4,128)S(1)} reshape(s32[16]{0:T(128)} %param.19) | data formatting | bytes 128 | tf_op jit(solution)/shard_map/lt | solution.py:327
  1.4 0.7 add_convert_fusion
  2.1 0.1 convert_element_type.20
  2.1 0.1 lt.40
  2.2 0.1 lt.43
  2.3 0.1 lt.44
  2.4 0.7 %broadcast_in_dim.10.idx_ref = s32[64,128]{1,0:T(8,128)S(1)} broadcast(s32[64]{0:T(128)} %bitcast.3), dimensions={0} | broadcast | bytes 33024 | tf_op jit(solution)/shard_map/broadcast_in_dim | solution.py:330
  3.1 0.2 negate_select_fusion
  3.3 0.0 copy-start
  3.4 1.2 %copy-done = bf16[4,64,2048]{2,1,0:T(8,128)(2,1)S(1)} copy-done((bf16[4,64,2048]{2,1,0:T(8,128)(2,1)S(1)}, bf16[4,64,2048]{2,1,0:T(8,128)(2,1)}, u32[]{:S(2)}) %copy-start) | copy-done | bytes 1048600
  4.6 0.0 copy-start.1
  4.6 1.2 %copy-done.1 = bf16[16,64,512]{2,1,0:T(8,128)(2,1)S(1)} copy-done((bf16[16,64,512]{2,1,0:T(8,128)(2,1)S(1)}, bf16[16,64,512]{2,1,0:T(8,128)(2,1)}, u32[]{:S(2)}) %copy-start.1) | copy-done | bytes 1048600
  5.8 0.0 copy-start.2
  5.8 1.2 %copy-done.2 = bf16[16,64,512]{2,1,0:T(8,128)(2,1)S(1)} copy-done((bf16[16,64,512]{2,1,0:T(8,128)(2,1)S(1)}, bf16[16,64,512]{2,1,0:T(8,128)(2,1)}, u32[]{:S(2)}) %copy-start.2) | copy-done | bytes 1048600
  7.0 0.0 copy-start.3
  7.0 1.0 %copy-done.3 = bf16[1,2048,128]{2,1,0:T(8,128)(2,1)S(1)} copy-done((bf16[1,2048,128]{2,1,0:T(8,128)(2,1)S(1)}, bf16[1,2048,128]{2,1,0:T(8,128)(2,1)}, u32[]{:S(2)}) %copy-start.3) | copy-done | bytes 524312
  8.1 0.0 copy-start.4
  8.1 1.0 %copy-done.4 = bf16[4,64,1024]{2,1,0:T(8,128)(2,1)S(1)} copy-done((bf16[4,64,1024]{2,1,0:T(8,128)(2,1)S(1)}, bf16[4,64,1024]{2,1,0:T(8,128)(2,1)}, u32[]{:S(2)}) %copy-start.4) | copy-done | bytes 524312
  9.1 0.9 %copy-done.5 = f32[128,272]{1,0:T(8,128)S(1)} copy-done((f32[128,272]{1,0:T(8,128)S(1)}, f32[128,272]{1,0:T(8,128)}, u32[]{:S(2)}) %copy-start.5) | copy-done | bytes 139288
  10.0 0.9 %copy-done.6 = bf16[1,2,64,512]{3,2,1,0:T(8,128)(2,1)S(1)} copy-done((bf16[1,2,64,512]{3,2,1,0:T(8,128)(2,1)S(1)}, bf16[1,2,64,512]{3,2,1,0:T(8,128)(2,1)}, u32[]{:S(2)}) %copy-start.6) | copy-done | bytes 131096
  10.9 0.7 %copy-done.7 = bf16[64,64]{1,0:T(8,128)(2,1)S(1)} copy-done((bf16[64,64]{1,0:T(8,128)(2,1)S(1)}, bf16[64,64]{1,0:T(8,128)(2,1)}, u32[]{:S(2)}) %copy-start.7) | copy-done | bytes 8216
  11.7 55.2 %shard_map.122 = (bf16[4,64,1024]{2,1,0:T(8,128)(2,1)S(1)}, bf16[4,16,1024]{2,1,0:T(8,128)(2,1)S(1)}) custom-call(s32[64,128]{1,0:T(8,128)S(1)} %broadcast_in_dim.10.idx_ref, f32[64,128]{1,0:T(8,128)S(1)} %get-tuple-element.3.cos_ref, f32[64,128]{1,0:T(8,128)S(1)} %get-tuple-element.2.sin_ref, f32[4,272]{1,0:T(4,128)S(1)} %pad_convert_fusion.colok_ref, ...), custom_call_target="tpu_custom_call" | custom-call | tf_op jit(solution)/shard_map/pallas_call | solution.py:344
  66.9 0.8 %copy.15 = bf16[4,64,1024]{2,1,0:T(8,128)(2,1)} copy(bf16[4,64,1024]{2,1,0:T(8,128)(2,1)S(1)} %get-tuple-element.6) | data formatting | bytes 1048576
  67.7 0.7 copy.16
  (8 shorter events, 0.0 us)
Async XLA Ops:
  3.3 1.2 %copy-start = (bf16[4,64,2048]{2,1,0:T(8,128)(2,1)S(1)}, bf16[4,64,2048]{2,1,0:T(8,128)(2,1)}, u32[]{:S(2)}) copy-start(bf16[4,64,2048]{2,1,0:T(8,128)(2,1)} %x_hbm.1) | copy-start | bytes 3145732
  4.6 1.2 %copy-start.1 = (bf16[16,64,512]{2,1,0:T(8,128)(2,1)S(1)}, bf16[16,64,512]{2,1,0:T(8,128)(2,1)}, u32[]{:S(2)}) copy-start(bf16[16,64,512]{2,1,0:T(8,128)(2,1)} %k_hbm.1) | copy-start | bytes 3145732
  5.8 1.2 %copy-start.2 = (bf16[16,64,512]{2,1,0:T(8,128)(2,1)S(1)}, bf16[16,64,512]{2,1,0:T(8,128)(2,1)}, u32[]{:S(2)}) copy-start(bf16[16,64,512]{2,1,0:T(8,128)(2,1)} %v_hbm.1) | copy-start | bytes 3145732
  7.0 1.0 %copy-start.3 = (bf16[1,2048,128]{2,1,0:T(8,128)(2,1)S(1)}, bf16[1,2048,128]{2,1,0:T(8,128)(2,1)}, u32[]{:S(2)}) copy-start(bf16[1,2048,128]{2,1,0:T(8,128)(2,1)} %a_hbm.1) | copy-start | bytes 1572868
  8.1 1.0 %copy-start.4 = (bf16[4,64,1024]{2,1,0:T(8,128)(2,1)S(1)}, bf16[4,64,1024]{2,1,0:T(8,128)(2,1)}, u32[]{:S(2)}) copy-start(bf16[4,64,1024]{2,1,0:T(8,128)(2,1)} %q_hbm.1) | copy-start | bytes 1572868
  9.1 0.9 %copy-start.5 = (f32[128,272]{1,0:T(8,128)S(1)}, f32[128,272]{1,0:T(8,128)}, u32[]{:S(2)}) copy-start(f32[128,272]{1,0:T(8,128)} %constant.31.clone.same_ref) | copy-start | bytes 417796
  10.0 0.9 %copy-start.6 = (bf16[1,2,64,512]{3,2,1,0:T(8,128)(2,1)S(1)}, bf16[1,2,64,512]{3,2,1,0:T(8,128)(2,1)}, u32[]{:S(2)}) copy-start(bf16[1,2,64,512]{3,2,1,0:T(8,128)(2,1)} %param.14) | copy-start | bytes 393220
  10.9 0.7 %copy-start.7 = (bf16[64,64]{1,0:T(8,128)(2,1)S(1)}, bf16[64,64]{1,0:T(8,128)(2,1)}, u32[]{:S(2)}) copy-start(bf16[64,64]{1,0:T(8,128)(2,1)} %constant.32.clone.perm_ref) | copy-start | bytes 24580

commit v2 on v1

--- a/solution.py
+++ b/solution.py
@@ -3,7 +3,6 @@
 
 import jax
 import jax.numpy as jnp
-import numpy as np
 from jax import lax
 from jax.experimental import pallas as pl
 from jax.experimental.pallas import tpu as pltpu
@@ -21,11 +20,11 @@
 
 def kernel(
     n_a, n_t, chunks,
-    idx_ref, cos_ref, sin_ref, colok_ref, same_ref, perm_ref,
+    idx_ref, len_ref,
     x_hbm, w_hbm, a_hbm, u_hbm, q_hbm, k_hbm, v_hbm,
     ctx_hbm, new_ref,
     x_ref, w_ref, down, up, k_ref, v_ref, q_all, qp,
-    part, base_in, shr, shr_in, newp, ctxs,
+    part, base_in, shr, shr_in, newp, ctxs, oc, mc, lc, idxs,
     loc, a_send, a_recv, u_send, u_recv, uz_send, uz_recv,
     q_send, q_recv, b_send, b_recv, s_send, s_recv, c_send, c_recv,
 ):
@@ -41,6 +40,19 @@
     hl = q_hbm.shape[2]
     hpt = hl // HD
 
+    cache = k_ref.shape[1]
+    per = 16 // steps
+    n0 = per * steps
+    tr = n0 * hpt
+    iota = lax.broadcasted_iota
+    I32 = jnp.int32
+    scale = 1.0 / math.sqrt(HD)
+
+    def column(row):
+        n = row.shape[1]
+        eye = iota(I32, (n, n), 0) == iota(I32, (n, n), 1)
+        return jnp.sum(jnp.where(eye, row.astype(F32), 0.0), axis=1, keepdims=True)
+
     x_cp = pltpu.make_async_copy(x_hbm, x_ref, loc.at[0])
     w_cp = pltpu.make_async_copy(w_hbm, w_ref, loc.at[1])
     a_cp = pltpu.make_async_copy(a_hbm.at[0], down.at[z], loc.at[2])
@@ -153,8 +165,51 @@
     for d in range(1, n_t):
         b_copy(d).start()
 
-    idx = jnp.concatenate([idx_ref[...]] * steps, axis=0)
     rank = down.shape[2]
+    idxs[...] = jnp.broadcast_to(column(idx_ref[...]).astype(I32), (rows, rank))
+    idx = jnp.concatenate([idxs[...]] * steps, axis=0)
+    i0 = iota(I32, (otile, otile), 0)
+    perm = jnp.where(
+        iota(I32, (otile, otile), 1) == (i0 % steps) * own + i0 // steps, 1.0, 0.0).astype(BF16)
+    lens = jnp.concatenate([column(len_ref[...])] * steps, axis=0)
+    lens_rs = jnp.dot(
+        perm, jnp.broadcast_to(lens, (otile, HD)).astype(BF16), preferred_element_type=F32).astype(I32)
+    pair = (iota(I32, (1, HD), 1) % (HD // 2)).astype(F32)
+    frequency = jnp.exp(-(2.0 * pair / HD) * math.log(500000.0))
+    angles = (lens + (iota(I32, (otile, 1), 0) // own).astype(F32)) * frequency
+    cosine = jnp.cos(angles)
+    sine = jnp.sin(angles)
+    sine = jnp.where(iota(I32, (otile, HD), 1) < HD // 2, -sine, sine)
+    row_of = iota(I32, (tr, per * cache), 0) % n0 // steps
+    col_at = iota(I32, (tr, per * cache), 1)
+    same_row = row_of == col_at // cache
+    col_p = col_at % cache
+    line2 = iota(I32, (tr, n0), 0) % n0
+    col2 = iota(I32, (tr, n0), 1)
+    same_new = (line2 // steps == col2 // steps) & (col2 % steps <= line2 % steps)
+
+    order = [n_t // 2] + [d for d in range(1, n_t) if d != n_t // 2] + [0]
+
+    def query_tile(to, lines):
+        return jnp.concatenate([qp[to, lines, h * HD:(h + 1) * HD] for h in range(hpt)], axis=0)
+
+    def over_cache(d):
+        to = lax.rem(t + d, n_t)
+        kl = pl.ds(pl.multiple_of(to * hpt // GROUP * HD, HD), HD)
+        for b in range(own // per):
+            keys = k_ref[pl.ds(b * per, per), :, kl].reshape(per * cache, HD)
+            vals = v_ref[pl.ds(b * per, per), :, kl].reshape(per * cache, HD)
+            sc = lax.dot_general(
+                query_tile(to, pl.ds(b * n0, n0)), keys, (((1,), (1,)), ((), ())),
+                preferred_element_type=F32) * scale
+            limit = jnp.concatenate([lens_rs[b * n0:(b + 1) * n0, :1]] * hpt, axis=0)
+            sc = jnp.where(same_row & (col_p < limit), sc, -1e30)
+            top = jnp.max(sc, axis=1, keepdims=True)
+            e = jnp.exp(sc - top)
+            at = d * (own // per) + b
+            mc[at] = jnp.broadcast_to(top, (tr, HD))
+            lc[at] = jnp.broadcast_to(jnp.sum(e, axis=1, keepdims=True), (tr, HD))
+            oc[at] = jnp.dot(e.astype(BF16), vals, preferred_element_type=F32)
 
     def shrink_part(a, lo, size):
         got = jnp.dot(
@@ -165,40 +220,13 @@
     shr[...] = shrink_part(z, 0, depth)
 
     for k in range(1, n_a):
-        for direction in range(2):
-            @pl.when(held(direction, k))
-            def _(direction=direction, k=k):
-                arrived_uz(direction, k)
-                a = z - k if direction == 0 else z + k
-                for d in range(1, n_t):
-                    u_copy(a, 2 * k - 1 + direction, d).start()
-
-            @pl.when(sends(direction, k))
-            def _(direction=direction, k=k):
-                uz_copy(direction, k).start()
-        for c in range(chunks):
-            for direction in range(2):
-                @pl.when(held(direction, k))
-                def _(direction=direction, k=k, c=c):
-                    arrived_a(direction, k, c)
-
-                @pl.when(sends(direction, k))
-                def _(direction=direction, k=k, c=c):
-                    a_copy(direction, k, c).start()
-
-            for direction in range(2):
-                @pl.when(held(direction, k))
-                def _(direction=direction, k=k, c=c):
-                    a = z - k if direction == 0 else z + k
-                    shr[...] += shrink_part(a, c * cd, cd)
-
-        if k == n_a - 2 or n_a == 2:
+        if k == n_a - 1:
             q_cp.wait()
             for d in range(1, n_t):
                 q_copy(d).wait()
             for j in range(n_t):
                 qp[j] = jnp.dot(
-                    perm_ref[...], q_all[j].reshape(otile, hl), preferred_element_type=F32).astype(BF16)
+                    perm, q_all[j].reshape(otile, hl), preferred_element_type=F32).astype(BF16)
             for d in range(1, n_t):
                 b_copy(d).wait()
             mine = pl.ds(pl.multiple_of(t * own, own), own)
@@ -209,6 +237,36 @@
             k_cp.wait()
             v_cp.wait()
 
+        for direction in range(2):
+            @pl.when(held(direction, k))
+            def _(direction=direction, k=k):
+                arrived_uz(direction, k)
+                a = z - k if direction == 0 else z + k
+                for d in range(1, n_t):
+                    u_copy(a, 2 * k - 1 + direction, d).start()
+
+            @pl.when(sends(direction, k))
+            def _(direction=direction, k=k):
+                uz_copy(direction, k).start()
+        for c in range(chunks):
+            if k == n_a - 1:
+                for d in order[c::chunks]:
+                    over_cache(d)
+            for direction in range(2):
+                @pl.when(held(direction, k))
+                def _(direction=direction, k=k, c=c):
+                    arrived_a(direction, k, c)
+
+                @pl.when(sends(direction, k))
+                def _(direction=direction, k=k, c=c):
+                    a_copy(direction, k, c).start()
+
+            for direction in range(2):
+                @pl.when(held(direction, k))
+                def _(direction=direction, k=k, c=c):
+                    a = z - k if direction == 0 else z + k
+                    shr[...] += shrink_part(a, c * cd, cd)
+
     for d in range(1, n_t):
         s_copy(d).start()
     for d in range(1, n_t):
@@ -228,10 +286,10 @@
         total = total + shr_in[d - 1]
     shrunk = total.reshape(otile, rank)
     both = jnp.concatenate([shrunk, shrunk], axis=0)
-    line = lax.broadcasted_iota(jnp.int32, (2 * otile, rank), 0)
-    lane = lax.broadcasted_iota(jnp.int32, (2 * otile, rank), 1)
+    line = iota(I32, (2 * otile, rank), 0)
+    lane = iota(I32, (2 * otile, rank), 1)
     both = jnp.where((line < otile) == (lane < rank // 2), both, 0.0)
-    idx_own = idx_ref[mine]
+    idx_own = idxs[mine]
     idx_both = jnp.concatenate([idx_own] * (2 * steps), axis=0)
     delta = jnp.zeros((2 * otile, KEY_VALUE_WIDTH), F32)
     for a in range(n_a):
@@ -243,11 +301,11 @@
     pieces = []
     for h in range(KV):
         one = fresh[:, h * HD:(h + 1) * HD] + delta[:otile, h * HD:(h + 1) * HD]
-        pieces.append(one * cos_ref[...] + pltpu.roll(one, HD // 2, 1) * sin_ref[...])
+        pieces.append(one * cosine + pltpu.roll(one, HD // 2, 1) * sine)
     pieces.append(fresh[:, KEY_VALUE_WIDTH:] + delta[otile:])
     new_kv = jnp.concatenate(pieces, axis=1).astype(BF16)
     new_ref[...] = new_kv.reshape(steps, own, width)
-    newp[...] = jnp.dot(perm_ref[...], new_kv, preferred_element_type=F32).astype(BF16)
+    newp[...] = jnp.dot(perm, new_kv, preferred_element_type=F32).astype(BF16)
 
     def c_copy(d):
         to = lax.rem(t + d, n_t)
@@ -255,9 +313,6 @@
             src_ref=ctxs.at[d], dst_ref=ctx_hbm.at[:, pl.ds(pl.multiple_of(t * own, own), own)],
             send_sem=c_send.at[d - 1], recv_sem=c_recv.at[d - 1], device_id={"tensor": to}, device_id_type=MESH)
 
-    per = same_ref.shape[1] // (k_ref.shape[1] + steps)
-    scale = 1.0 / math.sqrt(HD)
-    order = [n_t // 2] + [d for d in range(1, n_t) if d != n_t // 2] + [0]
     for d in order:
         to = lax.rem(t + d, n_t)
         g = to * hpt // GROUP
@@ -265,22 +320,22 @@
         vl = pl.ds(pl.multiple_of(KEY_VALUE_WIDTH + g * HD, HD), HD)
         tiles = []
         for b in range(own // per):
-            r0, n0 = b * per, per * steps
             lines = pl.ds(b * n0, n0)
-            qt = jnp.concatenate([qp[to, lines, h * HD:(h + 1) * HD] for h in range(hpt)], axis=0)
-            keys = jnp.concatenate(
-                [k_ref[pl.ds(r0, per), :, kl].reshape(per * k_ref.shape[1], HD), newp[lines, kl]], axis=0)
-            vals = jnp.concatenate(
-                [v_ref[pl.ds(r0, per), :, kl].reshape(per * v_ref.shape[1], HD), newp[lines, vl]], axis=0)
-            sc = lax.dot_general(qt, keys, (((1,), (1,)), ((), ())), preferred_element_type=F32) * scale
-            sc = jnp.where(same_ref[...] * colok_ref[pl.ds(b, 1), :] > 0, sc, -1e30)
-            e = jnp.exp(sc - jnp.max(sc, axis=1, keepdims=True))
-            tot = jnp.sum(e, axis=1, keepdims=True)
-            o = (jnp.dot(e.astype(BF16), vals, preferred_element_type=F32) / tot).astype(BF16)
+            at = d * (own // per) + b
+            sc = lax.dot_general(
+                query_tile(to, lines), newp[lines, kl], (((1,), (1,)), ((), ())),
+                preferred_element_type=F32) * scale
+            sc = jnp.where(same_new, sc, -1e30)
+            top = jnp.maximum(mc[at], jnp.max(sc, axis=1, keepdims=True))
+            e = jnp.exp(sc - top[:, :n0])
+            less = jnp.exp(mc[at] - top)
+            tot = lc[at] * less + jnp.sum(e, axis=1, keepdims=True)
+            o = oc[at] * less + jnp.dot(e.astype(BF16), newp[lines, vl], preferred_element_type=F32)
+            o = (o / tot).astype(BF16)
             tiles.append(jnp.concatenate([o[h * n0:(h + 1) * n0] for h in range(hpt)], axis=1))
         ctxp = jnp.concatenate(tiles, axis=0)
         ctxs[d] = lax.dot_general(
-            perm_ref[...], ctxp, (((0,), (0,)), ((), ())), preferred_element_type=F32
+            perm, ctxp, (((0,), (0,)), ((), ())), preferred_element_type=F32
         ).astype(BF16).reshape(steps, own, hl)
         if d:
             c_copy(d).start()
@@ -310,36 +365,14 @@
     otile = steps * own
     width = key_value_weight.shape[1]
     rank = adapter_down_weight.shape[2]
-    cache = stored_cache_keys.shape[1]
     hl = queries.shape[2]
     hpt = hl // HD
     per = 16 // steps
     chunks = 4
     uq = rank // n_t
 
-    i = np.arange(otile)
-    perm = np.zeros((otile, otile), np.float32)
-    perm[i, (i % steps) * own + i // steps] = 1
-    line = np.arange(hpt * per * steps) % (per * steps)
-    col_r = np.concatenate([np.repeat(np.arange(per), cache), np.repeat(np.arange(per), steps)])
-    col_s = np.concatenate([np.full(per * cache, -1), np.tile(np.arange(steps), per)])
-    same = (line[:, None] // steps == col_r[None]) & (col_s[None] <= line[:, None] % steps)
-    filled = (jnp.arange(cache, dtype=jnp.int32)[None] < filled_cache_length[:, None]).astype(F32)
-    colok = jnp.concatenate(
-        [filled.reshape(own // per, per * cache), jnp.ones((own // per, per * steps), F32)], axis=1)
-    idx = jnp.broadcast_to(request_adapter_index, (rows, rank))
-    positions = (
-        filled_cache_length[None, :] + jnp.arange(steps, dtype=jnp.int32)[:, None]
-    ).astype(F32).reshape(otile, 1)
-    half = HD // 2
-    pair = jnp.arange(HD, dtype=jnp.int32) % half
-    frequency = jnp.exp(-(2.0 * pair.astype(F32) / HD) * math.log(500000.0))
-    angles = positions * frequency[None]
-    cosine = jnp.cos(angles)
-    sine = jnp.where(jnp.arange(HD)[None] < half, -jnp.sin(angles), jnp.sin(angles))
-
     vm = pl.BlockSpec(memory_space=pltpu.VMEM)
-    hbm = pl.BlockSpec(memory_space=pl.ANY)
+    hbm = pl.BlockSpec(memory_space=pltpu.HBM)
     dma = pltpu.SemaphoreType.DMA
     context, new_kv = pl.pallas_call(
         functools.partial(kernel, n_a, n_t, chunks),
@@ -347,7 +380,7 @@
             jax.ShapeDtypeStruct((steps, rows, hl), BF16),
             jax.ShapeDtypeStruct((steps, own, width), BF16),
         ),
-        in_specs=[vm] * 6 + [hbm] * 7,
+        in_specs=[vm] * 2 + [hbm] * 7,
         out_specs=(hbm, vm),
         scratch_shapes=[
             pltpu.VMEM((steps, rows, depth), BF16),
@@ -364,6 +397,8 @@
             pltpu.VMEM((n_t - 1, steps, own, rank), F32),
             pltpu.VMEM((otile, width), BF16),
             pltpu.VMEM((n_t, steps, own, hl), BF16),
+            *[pltpu.VMEM((n_t * (own // per), hpt * per * steps, HD), F32)] * 3,
+            pltpu.VMEM((rows, rank), jnp.int32),
             dma((8,)),
             dma((2, n_a, chunks)), dma((2, n_a, chunks)),
             dma((2 * n_a, n_t - 1)), dma((2 * n_a, n_t - 1)),
@@ -374,9 +409,9 @@
             dma((n_t - 1,)), dma((n_t - 1,)),
         ],
         compiler_params=pltpu.CompilerParams(
-            collective_id=0, has_side_effects=True, vmem_limit_bytes=48 * 1024 * 1024),
+            collective_id=0, has_side_effects=True, vmem_limit_bytes=63 * 1024 * 1024),
     )(
-        idx, cosine, sine, colok, jnp.asarray(same, F32), jnp.asarray(perm, BF16),
+        request_adapter_index.reshape(1, rows), filled_cache_length.reshape(1, own),
         normed_layer_inputs, key_value_weight, adapter_down_weight,
         adapter_up_weight.reshape(n_t, uq, KEY_VALUE_WIDTH), queries,
         stored_cache_keys, stored_cache_values,

time: 68.8 us -> 59.9 us (0.87)
  local copies, waits for them, and re-layouts: 11.5 us -> 3.44 us
  other arithmetic: 0.89 us -> 0 us
    unnamed x18 -> x2, local copies, waits for them, and re-layouts: 9.75 us -> 3.44 us
    lt x5 -> x0, local copies, waits for them, and re-layouts: 0.98 us -> none  [body(): jnp.arange(cache, dtype=jnp.int32)[None] < filled_cache_length[:, None]]
    broadcast_in_dim x1 -> x0, local copies, waits for them, and re-layouts: 0.73 us -> none  [body(): idx = jnp.broadcast_to(request_adapter_index, (rows, rank))]
where the time goes in v2:
time: 59.9 us; the launch traced here: 59.7 us
  Pallas kernels  55.6 us (93%)
  local copies, waits for them, and re-layouts  3.44 us (6%)
  between operations  0.64 us (1%)
    pallas_call x1, Pallas kernels, body(): pl.pallas_call(functools.partial(kernel, n_a, n_t, chunks), out_shape=(ja...  55.6 us
    unnamed x2, local copies, waits for them, and re-layouts  3.44 us

profile of v2, /device:TPU:0, one launch (start us, length us, event | category | flops | bytes accessed | tf_op | source)
XLA Modules:
  0.0 59.7 jit_solution(12614172223214962338)
XLA Ops:
  0.6 55.6 %shard_map.104 = (bf16[4,64,1024]{2,1,0:T(8,128)(2,1)}, bf16[4,16,1024]{2,1,0:T(8,128)(2,1)}) custom-call(s32[1,64]{1,0:T(1,128)} %bitcast.4, s32[1,16]{1,0:T(1,128)} %bitcast.5, bf16[4,64,2048]{2,1,0:T(8,128)(2,1)} %x_hbm.1, bf16[2048,1024]{1,0:T(8,128)(2,1)} %w_hbm.1, bf16[1,2048,128]{2,1,0:T(8,128)(2,1)} %a_hbm.1, bf16[4,32,512]{2,1,0:T(8,128)(2,1)} %bitcast.3, ...), custom_call_target="tpu_custom_call" | custom-call | tf_op jit(solution)/shard_map/pallas_call | solution.py:377
  56.2 1.9 %copy.13 = bf16[4,64,1024]{2,1,0:T(8,128)(2,1)} copy(bf16[4,64,1024]{2,1,0:T(8,128)(2,1)} %get-tuple-element.4) | data formatting | bytes 1048576
  58.1 1.6 %copy.14 = bf16[4,16,1024]{2,1,0:T(8,128)(2,1)} copy(bf16[4,16,1024]{2,1,0:T(8,128)(2,1)} %get-tuple-element.5) | data formatting | bytes 262144

commit v3 on v2

--- a/solution.py
+++ b/solution.py
@@ -24,8 +24,8 @@
     x_hbm, w_hbm, a_hbm, u_hbm, q_hbm, k_hbm, v_hbm,
     ctx_hbm, new_ref,
     x_ref, w_ref, down, up, k_ref, v_ref, q_all, qp,
-    part, base_in, shr, shr_in, newp, ctxs, oc, mc, lc, idxs,
-    loc, a_send, a_recv, u_send, u_recv, uz_send, uz_recv,
+    part, base_in, shr, shr_in, newp, ctxs, oc, mc, lc, idxs, gx, gidx, gshr, gshr_in,
+    guest, loc, a_send, a_recv, u_send, u_recv, uz_send, uz_recv,
     q_send, q_recv, b_send, b_recv, s_send, s_recv, c_send, c_recv,
 ):
     z = lax.axis_index("adapter")
@@ -64,6 +64,30 @@
     for cp in (a_cp, u_cp, x_cp, w_cp, q_cp, k_cp, v_cp):
         cp.start()
 
+    rank = down.shape[2]
+    idxs[...] = jnp.broadcast_to(column(idx_ref[...]).astype(I32), (rows, rank))
+
+    gc = 3 if n_a >= 4 else 0
+    gs = gc * cd
+    is_end = jnp.logical_or(z == 0, z == n_a - 1)
+    is_host = jnp.logical_or(z == 1, z == n_a - 2)
+    host_of = jnp.where(z == 0, 1, n_a - 2)
+    end_of = jnp.where(z == 1, 0, n_a - 1)
+
+    def guest_copy(i, src, dst, to):
+        return pltpu.make_async_remote_copy(
+            src_ref=src, dst_ref=dst, send_sem=guest.at[2 * i], recv_sem=guest.at[2 * i + 1],
+            device_id={"adapter": to}, device_id_type=MESH)
+
+    def gx_copy():
+        return guest_copy(0, x_hbm.at[:, :, pl.ds(0, gs)], gx, host_of)
+
+    def gi_copy():
+        return guest_copy(1, idxs, gidx, host_of)
+
+    def gr_copy():
+        return guest_copy(2, gshr, gshr_in, end_of)
+
     barrier = pltpu.get_barrier_semaphore()
     for d in range(1, n_t):
         pl.semaphore_signal(barrier, inc=1, device_id={"tensor": lax.rem(t + d, n_t)}, device_id_type=MESH)
@@ -99,6 +123,16 @@
 
     def sends(direction, k):
         return jnp.logical_and(held(direction, k), z < n_a - 1 if direction == 0 else z > 0)
+
+    def arrives(direction, k, c):
+        if c >= gc:
+            return held(direction, k)
+        return jnp.logical_and(held(direction, k), z < n_a - 1 if direction == 0 else z > 0)
+
+    def a_sends(direction, k, c):
+        if c >= gc:
+            return sends(direction, k)
+        return jnp.logical_and(held(direction, k), z < n_a - 2 if direction == 0 else z > 1)
 
     def u_copy(a, slot, d):
         block = up.at[a, t]
@@ -124,9 +158,15 @@
     a_cp.wait()
     for c in range(chunks):
         for direction in range(2):
-            @pl.when(sends(direction, 0))
+            @pl.when(a_sends(direction, 0, c))
             def _(direction=direction, c=c):
                 a_copy(direction, 0, c).start()
+
+        if gc and c == chunks // 2 - 1:
+            @pl.when(is_end)
+            def _():
+                gi_copy().start()
+                gx_copy().start()
 
     def q_copy(d):
         to = lax.rem(t + d, n_t)
@@ -165,8 +205,6 @@
     for d in range(1, n_t):
         b_copy(d).start()
 
-    rank = down.shape[2]
-    idxs[...] = jnp.broadcast_to(column(idx_ref[...]).astype(I32), (rows, rank))
     idx = jnp.concatenate([idxs[...]] * steps, axis=0)
     i0 = iota(I32, (otile, otile), 0)
     perm = jnp.where(
@@ -220,13 +258,17 @@
     shr[...] = shrink_part(z, 0, depth)
 
     for k in range(1, n_a):
-        if k == n_a - 1:
+        if k == max(1, n_a - 2):
             q_cp.wait()
             for d in range(1, n_t):
                 q_copy(d).wait()
             for j in range(n_t):
                 qp[j] = jnp.dot(
                     perm, q_all[j].reshape(otile, hl), preferred_element_type=F32).astype(BF16)
+            k_cp.wait()
+            v_cp.wait()
+
+        if k == n_a - 1:
             for d in range(1, n_t):
                 b_copy(d).wait()
             mine = pl.ds(pl.multiple_of(t * own, own), own)
@@ -234,8 +276,6 @@
             for d in range(1, n_t):
                 total = total + base_in[d - 1]
             base_in[0] = total
-            k_cp.wait()
-            v_cp.wait()
 
         for direction in range(2):
             @pl.when(held(direction, k))
@@ -249,23 +289,46 @@
             def _(direction=direction, k=k):
                 uz_copy(direction, k).start()
         for c in range(chunks):
-            if k == n_a - 1:
-                for d in order[c::chunks]:
-                    over_cache(d)
             for direction in range(2):
-                @pl.when(held(direction, k))
+                @pl.when(arrives(direction, k, c))
                 def _(direction=direction, k=k, c=c):
                     arrived_a(direction, k, c)
 
-                @pl.when(sends(direction, k))
+                @pl.when(a_sends(direction, k, c))
                 def _(direction=direction, k=k, c=c):
                     a_copy(direction, k, c).start()
 
             for direction in range(2):
-                @pl.when(held(direction, k))
+                @pl.when(arrives(direction, k, c))
                 def _(direction=direction, k=k, c=c):
                     a = z - k if direction == 0 else z + k
                     shr[...] += shrink_part(a, c * cd, cd)
+
+            if k == max(1, n_a - 2):
+                for d in (order[c // 2::chunks // 2] if c % 2 else []):
+                    over_cache(d)
+                if gc and c == gc:
+                    @pl.when(is_host)
+                    def _():
+                        gi_copy().wait_recv()
+                        gx_copy().wait_recv()
+                        skip = end_of
+                        names = jnp.concatenate([gidx[...]] * steps, axis=0)
+                        total = jnp.zeros((tile, rank), F32)
+                        for i in range(n_a - 1):
+                            a = lax.rem(skip + 1 + i, n_a)
+                            got = jnp.dot(
+                                gx[...].reshape(tile, gs), down[a, pl.ds(0, gs)],
+                                preferred_element_type=F32)
+                            total = total + jnp.where(names == a, got, 0.0)
+                        gshr[...] = total.reshape(steps, rows, rank)
+                        gr_copy().start()
+
+    if gc:
+        @pl.when(is_end)
+        def _():
+            gr_copy().wait_recv()
+            shr[...] += gshr_in[...]
 
     for d in range(1, n_t):
         s_copy(d).start()
@@ -347,8 +410,21 @@
             @pl.when(sends(direction, k))
             def _(direction=direction, k=k):
                 uz_copy(direction, k).wait_send()
-                for c in range(chunks):
+
+            for c in range(chunks):
+                @pl.when(a_sends(direction, k, c))
+                def _(direction=direction, k=k, c=c):
                     a_copy(direction, k, c).wait_send()
+
+    if gc:
+        @pl.when(is_end)
+        def _():
+            gi_copy().wait_send()
+            gx_copy().wait_send()
+
+        @pl.when(is_host)
+        def _():
+            gr_copy().wait_send()
     own_cp.wait()
     for d in range(1, n_t):
         c_copy(d).wait()
@@ -368,7 +444,7 @@
     hl = queries.shape[2]
     hpt = hl // HD
     per = 16 // steps
-    chunks = 4
+    chunks = 8
     uq = rank // n_t
 
     vm = pl.BlockSpec(memory_space=pltpu.VMEM)
@@ -399,6 +475,10 @@
             pltpu.VMEM((n_t, steps, own, hl), BF16),
             *[pltpu.VMEM((n_t * (own // per), hpt * per * steps, HD), F32)] * 3,
             pltpu.VMEM((rows, rank), jnp.int32),
+            pltpu.VMEM((steps, rows, max(128, 3 * depth // 8)), BF16),
+            pltpu.VMEM((rows, rank), jnp.int32),
+            *[pltpu.VMEM((steps, rows, rank), F32)] * 2,
+            dma((6,)),
             dma((8,)),
             dma((2, n_a, chunks)), dma((2, n_a, chunks)),
             dma((2 * n_a, n_t - 1)), dma((2 * n_a, n_t - 1)),

time: 59.9 us -> 59.3 us (0.990)
  Pallas kernels: 55.6 us -> 55 us
where the time goes in v3:
time: 59.3 us; the launch traced here: 59.1 us
  Pallas kernels  55 us (93%)
  local copies, waits for them, and re-layouts  3.44 us (6%)
  between operations  0.64 us (1%)
    pallas_call x1, Pallas kernels, body(): pl.pallas_call(functools.partial(kernel, n_a, n_t, chunks), out_shape=(ja...  55 us
    unnamed x2, local copies, waits for them, and re-layouts  3.44 us

profile of v3, /device:TPU:0, one launch (start us, length us, event | category | flops | bytes accessed | tf_op | source)
XLA Modules:
  0.0 59.1 jit_solution(13674230600306324872)
XLA Ops:
  0.6 55.0 %shard_map.104 = (bf16[4,64,1024]{2,1,0:T(8,128)(2,1)}, bf16[4,16,1024]{2,1,0:T(8,128)(2,1)}) custom-call(s32[1,64]{1,0:T(1,128)} %bitcast.4, s32[1,16]{1,0:T(1,128)} %bitcast.5, bf16[4,64,2048]{2,1,0:T(8,128)(2,1)} %x_hbm.1, bf16[2048,1024]{1,0:T(8,128)(2,1)} %w_hbm.1, bf16[1,2048,128]{2,1,0:T(8,128)(2,1)} %a_hbm.1, bf16[4,32,512]{2,1,0:T(8,128)(2,1)} %bitcast.3, ...), custom_call_target="tpu_custom_call" | custom-call | tf_op jit(solution)/shard_map/pallas_call | solution.py:453
  55.7 1.9 %copy.13 = bf16[4,64,1024]{2,1,0:T(8,128)(2,1)} copy(bf16[4,64,1024]{2,1,0:T(8,128)(2,1)} %get-tuple-element.4) | data formatting | bytes 1048576
  57.5 1.6 %copy.14 = bf16[4,16,1024]{2,1,0:T(8,128)(2,1)} copy(bf16[4,16,1024]{2,1,0:T(8,128)(2,1)} %get-tuple-element.5) | data formatting | bytes 262144

commit v4 on v3

--- a/solution.py
+++ b/solution.py
@@ -304,10 +304,11 @@
                     a = z - k if direction == 0 else z + k
                     shr[...] += shrink_part(a, c * cd, cd)
 
-            if k == max(1, n_a - 2):
-                for d in (order[c // 2::chunks // 2] if c % 2 else []):
+            if k == n_a - 1:
+                for d in (order[c // 2::chunks // 2] if c % 2 == 0 else []):
                     over_cache(d)
-                if gc and c == gc:
+            if k == n_a - 2:
+                if gc and c == chunks - 1:
                     @pl.when(is_host)
                     def _():
                         gi_copy().wait_recv()
@@ -428,6 +429,17 @@
     own_cp.wait()
     for d in range(1, n_t):
         c_copy(d).wait()
+
+
+def hand_over(steps, ctx_in, new_in, ctx_out, new_out, sems):
+    copies = []
+    for i in range(steps):
+        copies.append(pltpu.make_async_copy(ctx_in.at[i], ctx_out.at[i], sems.at[2 * i]))
+        copies.append(pltpu.make_async_copy(new_in.at[i], new_out.at[i], sems.at[2 * i + 1]))
+    for cp in copies:
+        cp.start()
+    for cp in copies:
+        cp.wait()
 
 
 def body(
@@ -496,7 +508,15 @@
         adapter_up_weight.reshape(n_t, uq, KEY_VALUE_WIDTH), queries,
         stored_cache_keys, stored_cache_values,
     )
-    return (context, new_kv)
+    pieces = 2 * steps
+    return pl.pallas_call(
+        functools.partial(hand_over, steps),
+        out_shape=(
+            jax.ShapeDtypeStruct(context.shape, BF16), jax.ShapeDtypeStruct(new_kv.shape, BF16)),
+        in_specs=[hbm] * 2,
+        out_specs=(hbm, hbm),
+        scratch_shapes=[dma((pieces,))],
+    )(context, new_kv)
 
 
 def solution(mesh):

time: 59.3 us -> 76.6 us (1.29)
  Pallas kernels: 55 us -> 75.8 us
  local copies, waits for them, and re-layouts: 3.44 us -> 0 us
    pallas_call x0 -> x1, Pallas kernels: none -> 21 us  [body(): pl.pallas_call(functools.partial(hand_over, steps), out_shape=(jax.ShapeD...]
    unnamed x2 -> x0, local copies, waits for them, and re-layouts: 3.44 us -> none
where the time goes in v4:
time: 76.6 us; the launch traced here: 76.5 us
  Pallas kernels  75.8 us (99%)
    pallas_call x1, Pallas kernels, body(): pl.pallas_call(functools.partial(kernel, n_a, n_t, chunks), out_shape=(ja...  54.8 us
    pallas_call x1, Pallas kernels, body(): pl.pallas_call(functools.partial(hand_over, steps), out_shape=(jax.ShapeD...  21 us

profile of v4, /device:TPU:0, one launch (start us, length us, event | category | flops | bytes accessed | tf_op | source)
XLA Modules:
  0.0 76.5 jit_solution(2762988633480741662)
XLA Ops:
  0.6 54.8 %shard_map.104 = (bf16[4,64,1024]{2,1,0:T(8,128)(2,1)}, bf16[4,16,1024]{2,1,0:T(8,128)(2,1)}) custom-call(s32[1,64]{1,0:T(1,128)} %bitcast.4, s32[1,16]{1,0:T(1,128)} %bitcast.5, bf16[4,64,2048]{2,1,0:T(8,128)(2,1)} %x_hbm.1, bf16[2048,1024]{1,0:T(8,128)(2,1)} %w_hbm.1, bf16[1,2048,128]{2,1,0:T(8,128)(2,1)} %a_hbm.1, bf16[4,32,512]{2,1,0:T(8,128)(2,1)} %bitcast.3, ...), custom_call_target="tpu_custom_call" | custom-call | tf_op jit(solution)/shard_map/pallas_call | solution.py:465
  55.5 21.0 %shard_map.105 = (bf16[4,64,1024]{2,1,0:T(8,128)(2,1)}, bf16[4,16,1024]{2,1,0:T(8,128)(2,1)}) custom-call(bf16[4,64,1024]{2,1,0:T(8,128)(2,1)} %get-tuple-element.4.ctx_in, bf16[4,16,1024]{2,1,0:T(8,128)(2,1)} %get-tuple-element.5.new_in), custom_call_target="tpu_custom_call" | custom-call | tf_op jit(solution)/shard_map/pallas_call | solution.py:512
